TPU v7x, 256 devices: a whole 4x4x8 slice. The times are simulated.
256 devices in a mesh: seq: 128 (over x_lo, z, y, core), batch: 2 (over x_hi).
Axes of the slice: x: 4 (x_hi: 2, x_lo: 2; x = x_hi * 2 + x_lo), y: 4, z: 8, core: 2. Of those that a mesh axis runs over, the one named last changes fastest.
Arguments:
- queries: bfloat16 [8192, 1024], P(('batch', 'seq')), parts along dimension 0, may hold values from -8 to 8
- keys: bfloat16 [8192, 1024], P(('batch', 'seq')), parts along dimension 0, may hold values from -8 to 8
- values: bfloat16 [8192, 1024], P(('batch', 'seq')), parts along dimension 0, may hold values from -6 to 6
- cross_queries: bfloat16 [8192, 1024], P(('batch', 'seq')), parts along dimension 0, may hold values from -8 to 8
- text_states: bfloat16 [256, 128, 4096], P(('batch', 'seq')), parts along dimension 0, may hold values from -6 to 6
- cross_kv_weight: bfloat16 [4096, 2048], P('seq'), may hold values from -1 to 1
- owner: int32 [2], P('batch'), parts along dimension 0, may hold values from 0 to 127
- prompt_len: int32 [2], P('batch'), parts along dimension 0, may hold values from 16 to 128
Outputs:
- mixed: bfloat16 [8192, 1024], P(('batch', 'seq')), parts along dimension 0
There are 2 independent parts, one for each index of `batch`. A program takes and returns all parts, laid end to end along the dimension named above; an argument that names none is the same for every part. Nothing has to cross between parts.
Inputs may be any that keep to these rules, and one draw needn't show every extreme that they name: The owner is one seq index of the sample. `prompt_len`: at least one prompt token is valid.
All inputs are finite; a program needn't handle non-finite values.
Results may differ from a plain program's by a relative error of at most 0.0076.
Values may be sent and summed in bfloat16 or wider, within the bound.
A program may use at most 128 MiB of HBM per device.

v0:
```python
import math

import jax
import jax.numpy as jnp
from jax import lax
from jax.sharding import PartitionSpec as P

HEAD_DIM = 128
HEADS = 8


def spread(shard, axis, root):
    mine = lax.axis_index(axis) == root
    return lax.psum(jnp.where(mine, shard, jnp.zeros_like(shard)), axis)


def start_state(heads, count):
    return (
        jnp.full((heads, count), -1e30, jnp.float32),
        jnp.zeros((heads, count), jnp.float32),
        jnp.zeros((heads, count, HEAD_DIM), jnp.float32),
    )


def absorb(head_queries, running, key_block, value_block):
    score_scale = 1.0 / math.sqrt(HEAD_DIM)
    top_score, total, summed = running
    count = key_block.shape[0]
    heads = head_queries.shape[1]
    key_heads = key_block.reshape(count, heads, HEAD_DIM)
    value_heads = value_block.reshape(count, heads, HEAD_DIM)
    scores = (
        jnp.einsum("qhd,khd->hqk", head_queries, key_heads, preferred_element_type=jnp.float32)
        * score_scale
    )
    new_top = jnp.maximum(top_score, jnp.max(scores, axis=2))
    weights = jnp.exp(scores - new_top[:, :, None])
    total = jnp.sum(weights, axis=2)
    summed = jnp.einsum(
        "hqk,khd->hqd",
        weights.astype(jnp.bfloat16),
        value_heads,
        preferred_element_type=jnp.float32,
    )
    return (new_top, total, summed)


def finish(running):
    return running[2] / running[1][:, :, None]


def on_device(
    queries, keys, values, cross_queries, text_states, cross_kv_weight, owner, prompt_len
):
    tok_count = queries.shape[0]
    inner = HEADS * HEAD_DIM
    head_queries = queries.reshape(tok_count, HEADS, HEAD_DIM)
    running = absorb(
        head_queries,
        start_state(HEADS, tok_count),
        lax.all_gather(keys, "seq", axis=0, tiled=True),
        lax.all_gather(values, "seq", axis=0, tiled=True),
    )
    self_heads = finish(running)
    self_out = self_heads.transpose(1, 0, 2).reshape(tok_count, inner)
    row_count = cross_kv_weight.shape[0]
    prompt = spread(text_states[0], "seq", owner[0])
    columns = lax.dynamic_slice_in_dim(prompt, lax.axis_index("seq") * row_count, row_count, 1)
    partial_value = jnp.dot(columns, cross_kv_weight, preferred_element_type=jnp.float32)
    cross_kv = lax.psum(partial_value, "seq").astype(jnp.bfloat16)
    prompt_rows = cross_kv.shape[0]
    cross_keys = cross_kv[:, :inner].reshape(prompt_rows, HEADS, HEAD_DIM)
    cross_values = cross_kv[:, inner:].reshape(prompt_rows, HEADS, HEAD_DIM)
    cross_heads_in = cross_queries.reshape(tok_count, HEADS, HEAD_DIM)
    score_scale = 1.0 / math.sqrt(HEAD_DIM)
    scores = (
        jnp.einsum("qhd,khd->hqk", cross_heads_in, cross_keys, preferred_element_type=jnp.float32)
        * score_scale
    )
    valid_mask = jnp.arange(prompt_rows, dtype=jnp.int32) < prompt_len[0]
    scores = jnp.where(valid_mask[None, None, :], scores, -1e30)
    top_score = jnp.max(scores, axis=2, keepdims=True)
    weights = jnp.exp(scores - top_score)
    total = jnp.sum(weights, axis=2, keepdims=True)
    cross_heads = (
        jnp.einsum(
            "hqk,khd->hqd",
            weights.astype(jnp.bfloat16),
            cross_values,
            preferred_element_type=jnp.float32,
        )
        / total
    )
    cross_out = cross_heads.transpose(1, 0, 2).reshape(tok_count, inner)
    return (self_out + cross_out).astype(jnp.bfloat16)


def solution(mesh):
    return jax.shard_map(
        on_device,
        mesh=mesh,
        in_specs=(
            P(("batch", "seq"), None),
            P(("batch", "seq"), None),
            P(("batch", "seq"), None),
            P(("batch", "seq"), None),
            P(("batch", "seq"), None, None),
            P("seq", None),
            P("batch"),
            P("batch"),
        ),
        out_specs=P(("batch", "seq"), None),
        check_vma=False,
    )
```

profile of v0, /device:TPU:1, one launch (start us, length us, event | category | flops | bytes accessed | tf_op | source)
XLA Modules:
  0.0 1691.8 jit_solution(10179562752613311533)
XLA Ops:
  6.5 0.0 copy-start
  7.2 1.1 select_bitcast_fusion
  8.3 0.0 all-reduce.3.cloned.1.call-update
  8.4 0.0 all-gather.3.cloned.1.call-start
  8.4 0.7 all-gather.3.cloned.1.call-update
  9.1 0.0 all-gather.5.cloned.1.call-start
  9.2 0.7 all-gather.5.cloned.1.call-update
  10.5 1079.9 %all-reduce.3.cloned.1.call-done = bf16[128,4096]{1,0:T(8,128)(2,1)} async-done(((bf16[128,4096]{1,0:T(8,128)(2,1)}), bf16[128,4096]{1,0:T(8,128)(2,1)}) %all-reduce.3.cloned.1.call-update) | async-done | bytes 1048592 | tf_op jit(solution)/shard_map/psum | solution.py:14
  1090.5 1.1 fusion.29
  1091.5 554.5 %all-reduce.4 = bf16[128,2048]{1,0:T(8,128)(2,1)S(1)} all-reduce(f32[128,2048]{1,0:T(8,128)S(1)} %fusion.29), channel_id=1, replica_groups=mesh['seq'=128,'batch'=2] {'seq'}, use_global_device_ids=true, to_apply=%region_3.4 | all-reduce | flops 262144 | bytes 1572864 | tf_op jit(solution)/shard_map/psum | solution.py:70
  1646.1 0.0 copy-done.3
  1646.1 0.3 fusion.33
  1646.4 0.2 fusion.21
  1646.6 0.0 copy-start.2
  1646.6 0.0 all-gather.3.cloned.1.call-done
  1646.6 11.3 copy.22
  1657.9 0.0 copy-done.2
  1657.9 4.7 fusion.32
  1662.6 1.9 copy-done.1
  1664.5 0.7 fusion
  1665.2 11.5 copy.25
  1676.7 7.7 fusion.8
  1684.4 0.3 fusion.16
  1684.7 0.6 copy.61
  (8 shorter events, 0.1 us)
Async XLA Ops:
  6.5 1083.9 %copy-start = (bf16[32,2048]{1,0:T(8,128)(2,1)S(1)}, bf16[32,2048]{1,0:T(8,128)(2,1)}, u32[]{:S(2)}) copy-start(bf16[32,2048]{1,0:T(8,128)(2,1)} %param.13) | copy-start | bytes 393220
  6.5 1639.5 %copy-start.3 = (bf16[32,1024]{1,0:T(8,128)(2,1)S(1)}, bf16[32,1024]{1,0:T(8,128)(2,1)}, u32[]{:S(2)}) copy-start(bf16[32,1024]{1,0:T(8,128)(2,1)} %param.11) | copy-start | bytes 196612
  6.5 1083.9 %all-reduce.3.cloned.1.call-start = ((), (), s32[]{:S(2)}) async-start(), calls=%async_computation.2 | async-start | bytes 2097152 | tf_op jit(solution)/shard_map/psum | solution.py:14
  8.4 1638.3 %all-gather.3.cloned.1.call-start = ((), (), s32[]{:S(2)}) async-start(), calls=%async_computation | async-start | bytes 8454144 | tf_op jit(solution)/shard_map/all_gather | solution.py:61
  9.1 1656.1 %all-gather.5.cloned.1.call-start = ((), (), s32[]{:S(2)}) async-start(), calls=%async_computation.1 | async-start | bytes 8454144 | tf_op jit(solution)/shard_map/all_gather | solution.py:62
  1646.6 11.3 copy-start.2
  1662.6 1.9 copy-start.1
Sparse Core Ops, SparseCore 0:
  10.0 1080.4 all-reduce.2
  1092.5 217.7 all-gather.2
  1312.3 218.3 all-gather.4
where the time goes:
time: 1700 us; the launch traced here: 1690 us
  waiting for transfers between devices  1080 us (64%)
  blocking collectives  554 us (33%)
  local copies, waits for them, and re-layouts  25.4 us (1%)
    psum x1, waiting for transfers between devices, spread(): return lax.psum(jnp.where(mine, shard, jnp.zeros_like(shard)), axis)  1080 us
    psum x1, blocking collectives, on_device(): cross_kv = lax.psum(partial_value, 'seq').astype(jnp.bfloat16)  554 us
  transfers between devices with their start and end apart: 3, of which 1 were waited for; matrix products, arithmetic and copies ran while one was open for 1% of the time, Pallas kernels for 0%

commit v1 on v0

v1 whole, which is shorter than its diff:
```python
import math

import jax
import jax.numpy as jnp
from jax import lax
from jax.experimental import pallas as pl
from jax.experimental.pallas import tpu as pltpu
from jax.sharding import PartitionSpec as P

HEAD_DIM = 128
HEADS = 8
NX, NZ, NY, NC = 2, 8, 4, 2
PLANE = NX * NY
TOK = 32
SLOT = TOK * NZ
SCALE = 1.0 / math.sqrt(HEAD_DIM)
F32 = jnp.float32
BF16 = jnp.bfloat16


def index_of(x, z, y, core):
    return ((x * NZ + z) * NY + y) * NC + core


def send(src, dst, send_sem, recv_sem, x, z, y, core):
    pltpu.make_async_remote_copy(
        src_ref=src,
        dst_ref=dst,
        send_sem=send_sem,
        recv_sem=recv_sem,
        device_id={"seq": index_of(x, z, y, core)},
        device_id_type=pl.DeviceIdType.MESH,
    ).start()


def local(src, dst, sem):
    pltpu.make_async_copy(src, dst, sem).start()


def wait_bytes(ref, sem):
    pltpu.make_async_copy(ref, ref, sem).wait()


def head_columns(head):
    return pl.ds(pl.multiple_of(head * HEAD_DIM, HEAD_DIM), HEAD_DIM)


def rows(start, count):
    return pl.ds(pl.multiple_of(start, count), count)


def dot_last(a, b):
    return lax.dot_general(a, b, (((1,), (1,)), ((), ())), preferred_element_type=F32)


def dot_first(a, b):
    return lax.dot_general(a, b, (((0,), (0,)), ((), ())), preferred_element_type=F32)


def kernel(
    owner_ref,
    len_ref,
    q_hbm,
    k_hbm,
    v_hbm,
    cq_hbm,
    text_hbm,
    w_hbm,
    out_ref,
    slots,
    piece_out,
    pieces,
    sub_out,
    subs,
    sub_mine,
    prompt,
    weight,
    kv,
    queries,
    cross_q,
    part_out,
    parts,
    row_mine,
    cross_kv,
    acc_out,
    accs,
    stat_out,
    stats,
    out_rows,
    ss,
    rs,
    kv_rs,
    acc_rs,
    stat_rs,
):
    me = lax.axis_index("seq")
    core = me % NC
    y = (me // NC) % NY
    z = (me // (NC * NY)) % NZ
    x = me // (NC * NY * NZ)
    f = x * NY + y
    xc = x * NC + core
    other = 1 - core

    local(text_hbm.at[0, rows(core * 64, 64), :], slots.at[core], rs.at[0])
    local(k_hbm.at[:, head_columns(z)], kv.at[y, 0, rows(z * TOK, TOK), :], rs.at[1])
    local(v_hbm.at[:, head_columns(z)], kv.at[y, 1, rows(z * TOK, TOK), :], rs.at[1])
    local(q_hbm.at[:, head_columns(z)], queries.at[xc, rows(z * TOK, TOK), :], rs.at[2])
    local(cq_hbm.at[:, head_columns(z)], cross_q.at[rows(z * TOK, TOK), :], rs.at[3])
    my_weight = rows((z * NC + core) * TOK, TOK)
    local(w_hbm.at[:, head_columns(core * HEADS + z)], weight.at[my_weight, :], rs.at[4])

    barrier = pltpu.get_barrier_semaphore()

    def greet_line(t, carry):
        p = (z * NC + core + t) % (NZ * NC)
        pl.semaphore_signal(
            barrier, inc=1, device_id={"seq": index_of(x, p // NC, y, p % NC)}, device_id_type=pl.DeviceIdType.MESH
        )
        return carry

    def greet_plane(t, carry):
        p = (f + t) % PLANE
        for c in range(NC):
            pl.semaphore_signal(
                barrier, inc=1, device_id={"seq": index_of(p // NY, z, p % NY, c)}, device_id_type=pl.DeviceIdType.MESH
            )
        return carry

    lax.fori_loop(1, NZ * NC, greet_line, 0)
    lax.fori_loop(1, PLANE, greet_plane, 0)
    pl.semaphore_wait(barrier, NZ * NC - 1 + (PLANE - 1) * NC)

    send(text_hbm.at[0, rows(other * 64, 64), :], slots.at[core], ss.at[0], rs.at[0], x, z, y, other)

    def line_kv(t, carry):
        zz = (z + t) % NZ
        send(k_hbm.at[:, head_columns(zz)], kv.at[y, 0, rows(z * TOK, TOK), :], ss.at[1], rs.at[1], x, zz, y, core)
        send(v_hbm.at[:, head_columns(zz)], kv.at[y, 1, rows(z * TOK, TOK), :], ss.at[1], rs.at[1], x, zz, y, core)
        return carry

    def line_q(t, carry):
        zz = (z + t) % NZ
        send(q_hbm.at[:, head_columns(zz)], queries.at[xc, rows(z * TOK, TOK), :], ss.at[2], rs.at[2], x, zz, y, core)
        return carry

    def line_cq(t, carry):
        zz = (z + t) % NZ
        send(cq_hbm.at[:, head_columns(zz)], cross_q.at[rows(z * TOK, TOK), :], ss.at[3], rs.at[3], x, zz, y, core)
        return carry

    def line_w(t, carry):
        p = (z * NC + core + t) % (NZ * NC)
        zz, cc = p // NC, p % NC
        send(w_hbm.at[:, head_columns(cc * HEADS + zz)], weight.at[my_weight, :], ss.at[4], rs.at[4], x, zz, y, cc)
        return carry

    lax.fori_loop(1, NZ, line_kv, 0)
    lax.fori_loop(1, NZ, line_q, 0)

    owner = owner_ref[0]
    wait_bytes(slots, rs.at[0])
    for fx in range(NX):
        for yp in range(NY // 2):
            for zp in range(NZ // 2):
                base = fx * (NZ * 256) + zp * 512 + yp * 128
                a = slots[owner % NC, :, base : base + 128]
                b = slots[owner % NC, :, base + 256 : base + 384]
                piece_out[fx * NY + 2 * yp, :, zp * 128 : zp * 128 + 128] = jnp.concatenate(
                    [a[:, :64], b[:, :64]], axis=1
                )
                piece_out[fx * NY + 2 * yp + 1, :, zp * 128 : zp * 128 + 128] = jnp.concatenate(
                    [a[:, 64:], b[:, 64:]], axis=1
                )
    local(piece_out.at[f], pieces.at[f], rs.at[5])

    def plane_pieces(t, carry):
        p = (f + t) % PLANE
        send(piece_out.at[p], pieces.at[f], ss.at[5], rs.at[5], p // NY, z, p % NY, core)
        return carry

    lax.fori_loop(1, PLANE, plane_pieces, 0)
    lax.fori_loop(1, NZ * NC, line_w, 0)

    wait_bytes(kv.at[0], rs.at[1])
    for t in range(1, NY):
        send(kv.at[y], kv.at[y], ss.at[6], kv_rs.at[t - 1], x, z, (y + t) % NY, core)
    wait_bytes(queries.at[0], rs.at[2])
    for t in range(1, NX * NC):
        p = (xc + t) % (NX * NC)
        send(queries.at[xc], queries.at[xc], ss.at[7], rs.at[6], p // NC, z, y, p % NC)
    lax.fori_loop(1, NZ, line_cq, 0)

    wait_bytes(pieces, rs.at[5])
    piece = pieces[(owner // (NC * NY * NZ)) * NY + (owner // NC) % NY]
    for r in range(4):
        for c in range(2):
            sub_out[r * 2 + c] = piece[r * 16 : r * 16 + 16, c * 256 : c * 256 + 256]
    local(sub_out.at[z], subs.at[z], rs.at[7])

    def line_subs(t, carry):
        zz = (z + t) % NZ
        send(sub_out.at[zz], subs.at[z], ss.at[8], rs.at[7], x, zz, y, core)
        return carry

    lax.fori_loop(1, NZ, line_subs, 0)

    for t in range(1, NY):
        wait_bytes(kv.at[0], kv_rs.at[t - 1])
    wait_bytes(queries.at[pl.ds(0, 3)], rs.at[6])

    def self_part(s):
        keys = kv[:, 0].reshape(NY * SLOT, HEAD_DIM)
        values = kv[:, 1].reshape(NY * SLOT, HEAD_DIM)
        scores = dot_last(keys, queries[s]) * SCALE
        top = jnp.max(scores, axis=0, keepdims=True)
        weights = jnp.exp(scores - top)
        total = jnp.sum(weights, axis=0, keepdims=True)
        acc = dot_first(values, weights.astype(BF16)) / total
        return acc.astype(BF16), top, total

    def self_send(t):
        p = (xc + t) % (NX * NC)
        acc, top, total = self_part(p)
        acc_out[p] = acc
        stat_out[p, 0:1, :] = top
        stat_out[p, 1:2, :] = total
        send(acc_out.at[p], accs.at[xc], ss.at[9], acc_rs.at[t - 1], p // NC, z, y, p % NC)
        send(stat_out.at[p], stats.at[xc], ss.at[10], stat_rs.at[t - 1], p // NC, z, y, p % NC)

    self_send(1)

    wait_bytes(subs, rs.at[7])
    sub_mine[...] = subs[(owner // (NC * NY)) % NZ]
    my_sub = prompt.at[z % 2, rows((core * 4 + z // 2) * 16, 16), :]
    local(sub_mine, my_sub, rs.at[8])

    def line_prompt(t, carry):
        p = (z * NC + core + t) % (NZ * NC)
        send(sub_mine, my_sub, ss.at[11], rs.at[8], x, p // NC, y, p % NC)
        return carry

    lax.fori_loop(1, NZ * NC, line_prompt, 0)

    self_send(2)

    wait_bytes(weight, rs.at[4])
    wait_bytes(prompt, rs.at[8])
    part = jnp.dot(prompt[0], weight[0:256], preferred_element_type=F32)
    part = part + jnp.dot(prompt[1], weight[256:512], preferred_element_type=F32)
    part_out[...] = part.reshape(PLANE, 16, HEAD_DIM)
    local(part_out.at[f], parts.at[f], rs.at[9])

    def plane_parts(t, carry):
        p = (f + t) % PLANE
        send(part_out.at[p], parts.at[f], ss.at[12], rs.at[9], p // NY, z, p % NY, core)
        return carry

    lax.fori_loop(1, PLANE, plane_parts, 0)

    self_send(3)
    acc, top, total = self_part(xc)
    accs[xc] = acc
    stats[xc, 0:1, :] = top
    stats[xc, 1:2, :] = total

    wait_bytes(parts, rs.at[9])
    row_mine[...] = jnp.sum(parts[...], axis=0).astype(BF16)
    my_rows = cross_kv.at[core, rows(f * 16, 16), :]
    local(row_mine, my_rows, rs.at[10])

    def plane_rows(t, carry):
        p = (f * NC + core + t) % (PLANE * NC)
        pf = p // NC
        send(row_mine, my_rows, ss.at[13], rs.at[10], pf // NY, z, pf % NY, p % NC)
        return carry

    lax.fori_loop(1, PLANE * NC, plane_rows, 0)

    for t in range(1, NX * NC):
        wait_bytes(accs.at[0], acc_rs.at[t - 1])
        wait_bytes(stats.at[0], stat_rs.at[t - 1])
    tops = [stats[s, 0:1, :] for s in range(NX * NC)]
    top = jnp.maximum(jnp.maximum(tops[0], tops[1]), jnp.maximum(tops[2], tops[3]))
    shares = [stats[s, 1:2, :] * jnp.exp(tops[s] - top) for s in range(NX * NC)]
    whole = shares[0] + shares[1] + shares[2] + shares[3]
    mixed = jnp.zeros((HEAD_DIM, SLOT), F32)
    for s in range(NX * NC):
        mixed = mixed + accs[s].astype(F32) * (shares[s] / whole)

    wait_bytes(cross_q, rs.at[3])
    wait_bytes(cross_kv, rs.at[10])
    scores = dot_last(cross_kv[0], cross_q[...]) * SCALE
    valid = lax.broadcasted_iota(jnp.int32, scores.shape, 0) < len_ref[0]
    scores = jnp.where(valid, scores, -1e30)
    weights = jnp.exp(scores - jnp.max(scores, axis=0, keepdims=True))
    total = jnp.sum(weights, axis=0, keepdims=True)
    mixed = mixed + dot_first(cross_kv[1], weights.astype(BF16)) / total
    out_rows[...] = mixed.T.astype(BF16)

    local(out_rows.at[rows(z * TOK, TOK), :], out_ref.at[:, head_columns(z)], rs.at[11])

    def line_out(t, carry):
        zz = (z + t) % NZ
        send(out_rows.at[rows(zz * TOK, TOK), :], out_ref.at[:, head_columns(z)], ss.at[14], rs.at[11], x, zz, y, core)
        return carry

    lax.fori_loop(1, NZ, line_out, 0)

    wait_bytes(slots.at[0], ss.at[0])
    wait_bytes(kv.at[0, :, pl.ds(0, 224), :], ss.at[1])
    wait_bytes(queries.at[0, pl.ds(0, 224), :], ss.at[2])
    wait_bytes(queries.at[0, pl.ds(0, 224), :], ss.at[3])
    wait_bytes(weight.at[pl.ds(0, 480), :], ss.at[4])
    wait_bytes(pieces.at[pl.ds(0, 7)], ss.at[5])
    wait_bytes(kv.at[pl.ds(0, 3)], ss.at[6])
    wait_bytes(queries.at[pl.ds(0, 3)], ss.at[7])
    wait_bytes(subs.at[pl.ds(0, 7)], ss.at[8])
    wait_bytes(accs.at[pl.ds(0, 3)], ss.at[9])
    wait_bytes(stats.at[pl.ds(0, 3)], ss.at[10])
    wait_bytes(weight.at[pl.ds(0, 480), :], ss.at[11])
    wait_bytes(parts.at[pl.ds(0, 7)], ss.at[12])
    wait_bytes(cross_q.at[pl.ds(0, 240), :], ss.at[13])
    wait_bytes(cross_q.at[pl.ds(0, 224), :], ss.at[14])
    wait_bytes(out_ref, rs.at[11])


def on_device(queries, keys, values, cross_queries, text_states, cross_kv_weight, owner, prompt_len):
    smem = pl.BlockSpec(memory_space=pltpu.SMEM)
    hbm = pl.BlockSpec(memory_space=pltpu.HBM)
    return pl.pallas_call(
        kernel,
        out_shape=jax.ShapeDtypeStruct((TOK, HEADS * HEAD_DIM), BF16),
        in_specs=[smem, smem] + [hbm] * 6,
        out_specs=pl.BlockSpec(memory_space=pltpu.VMEM),
        scratch_shapes=[
            pltpu.VMEM((NC, 64, 4096), BF16),
            pltpu.VMEM((PLANE, 64, 512), BF16),
            pltpu.VMEM((PLANE, 64, 512), BF16),
            pltpu.VMEM((NZ, 16, 256), BF16),
            pltpu.VMEM((NZ, 16, 256), BF16),
            pltpu.VMEM((16, 256), BF16),
            pltpu.VMEM((2, 128, 256), BF16),
            pltpu.VMEM((512, HEAD_DIM), BF16),
            pltpu.VMEM((NY, 2, SLOT, HEAD_DIM), BF16),
            pltpu.VMEM((NX * NC, SLOT, HEAD_DIM), BF16),
            pltpu.VMEM((SLOT, HEAD_DIM), BF16),
            pltpu.VMEM((PLANE, 16, HEAD_DIM), F32),
            pltpu.VMEM((PLANE, 16, HEAD_DIM), F32),
            pltpu.VMEM((16, HEAD_DIM), BF16),
            pltpu.VMEM((2, 128, HEAD_DIM), BF16),
            pltpu.VMEM((NX * NC, HEAD_DIM, SLOT), BF16),
            pltpu.VMEM((NX * NC, HEAD_DIM, SLOT), BF16),
            pltpu.VMEM((NX * NC, 8, SLOT), F32),
            pltpu.VMEM((NX * NC, 8, SLOT), F32),
            pltpu.VMEM((SLOT, HEAD_DIM), BF16),
            pltpu.SemaphoreType.DMA((15,)),
            pltpu.SemaphoreType.DMA((12,)),
            pltpu.SemaphoreType.DMA((NY - 1,)),
            pltpu.SemaphoreType.DMA((NX * NC - 1,)),
            pltpu.SemaphoreType.DMA((NX * NC - 1,)),
        ],
        compiler_params=pltpu.CompilerParams(
            collective_id=0, has_side_effects=True, vmem_limit_bytes=56 * 1024 * 1024
        ),
        cost_estimate=pl.CostEstimate(flops=700_000_000, bytes_accessed=2_000_000, transcendentals=1_100_000),
    )(owner, prompt_len, queries, keys, values, cross_queries, text_states, cross_kv_weight)


def solution(mesh):
    return jax.shard_map(
        on_device,
        mesh=mesh,
        in_specs=(
            P(("batch", "seq"), None),
            P(("batch", "seq"), None),
            P(("batch", "seq"), None),
            P(("batch", "seq"), None),
            P(("batch", "seq"), None, None),
            P("seq", None),
            P("batch"),
            P("batch"),
        ),
        out_specs=P(("batch", "seq"), None),
        check_vma=False,
    )
```

time: 1700 us -> 50.6 us (0.03)
  waiting for transfers between devices: 1080 us -> 0 us
  blocking collectives: 554 us -> 0 us
  Pallas kernels: 0 us -> 47.7 us
  local copies, waits for them, and re-layouts: 25.4 us -> 1.47 us
    psum x1 -> x0, waiting for transfers between devices: 1080 us -> none  [spread(): return lax.psum(jnp.where(mine, shard, jnp.zeros_like(shard)), axis)]
    psum x1 -> x0, blocking collectives: 554 us -> none  [on_device(): cross_kv = lax.psum(partial_value, 'seq').astype(jnp.bfloat16)]
    pallas_call x0 -> x1, Pallas kernels: none -> 47.7 us  [on_device(): pl.pallas_call(kernel, out_shape=jax.ShapeDtypeStruct((TOK, HEADS * HEAD_...]
    all_gather x2 -> x0, local copies, waits for them, and re-layouts: 22.8 us -> none  [the longest x1 11.5 us: on_device(): lax.all_gather(values, 'seq', axis=0, tiled=True)]
  transfers between devices with their start and end apart: 3 -> 0, of which waited for: 1 -> 0; matrix products, arithmetic and copies ran while one was open for 1% -> 0% of each run, Pallas kernels for 0% -> 0%
where the time goes in v1:
time: 50.6 us; the launch traced here: 50.5 us
  Pallas kernels  47.7 us (94%)
  local copies, waits for them, and re-layouts  1.47 us (3%)
  between operations  1.3 us (3%)
    pallas_call x1, Pallas kernels, on_device(): pl.pallas_call(kernel, out_shape=jax.ShapeDtypeStruct((TOK, HEADS * HEAD_...  47.7 us
    unnamed x1, local copies, waits for them, and re-layouts  1.47 us

profile of v1, /device:TPU:1, one launch (start us, length us, event | category | flops | bytes accessed | tf_op | source)
XLA Modules:
  0.0 50.5 jit_solution(615046582156870421)
XLA Ops:
  1.3 47.7 %shard_map.82 = bf16[32,1024]{1,0:T(8,128)(2,1)} custom-call(s32[1]{0:T(128)S(6)} %copy.10.owner_ref, s32[1]{0:T(128)S(6)} %copy.11.len_ref, bf16[32,1024]{1,0:T(8,128)(2,1)} %q_hbm.1, bf16[32,1024]{1,0:T(8,128)(2,1)} %k_hbm.1, bf16[32,1024]{1,0:T(8,128)(2,1)} %v_hbm.1, bf16[32,1024]{1,0:T(8,128)(2,1)} %cq_hbm.1, bf16[1,128,4096]{2,1,0:T(8,128)(2,1)} %text_hbm.1, ...), custom_call_target="tpu_custom_call" | custom-call | flops 700000000 | bytes 2000000 | tf_op jit(solution)/shard_map/pallas_call | solution.py:331
  49.0 1.5 %copy.12 = bf16[32,1024]{1,0:T(8,128)(2,1)} copy(bf16[32,1024]{1,0:T(8,128)(2,1)} %shard_map.82) | data formatting | bytes 131072

commit v2 on v1

v2 whole, which is shorter than its diff:
```python
import math

import jax
import jax.numpy as jnp
from jax import lax
from jax.experimental import pallas as pl
from jax.experimental.pallas import tpu as pltpu
from jax.sharding import PartitionSpec as P

HEAD_DIM = 128
HEADS = 8
NX, NZ, NY, NC = 2, 8, 4, 2
PLANE = NX * NY
TOK = 32
SLOT = TOK * NZ
SCALE = math.log2(math.e) / math.sqrt(HEAD_DIM)
HALF = 64
F32 = jnp.float32
BF16 = jnp.bfloat16


def index_of(x, z, y, core):
    return ((x * NZ + z) * NY + y) * NC + core


def send(src, dst, send_sem, recv_sem, x, z, y, core):
    pltpu.make_async_remote_copy(
        src_ref=src,
        dst_ref=dst,
        send_sem=send_sem,
        recv_sem=recv_sem,
        device_id={"seq": index_of(x, z, y, core)},
        device_id_type=pl.DeviceIdType.MESH,
    ).start()


def local(src, dst, sem):
    pltpu.make_async_copy(src, dst, sem).start()


def wait_bytes(ref, sem):
    pltpu.make_async_copy(ref, ref, sem).wait()


def head_columns(head):
    return pl.ds(pl.multiple_of(head * HEAD_DIM, HEAD_DIM), HEAD_DIM)


def rows(start, count):
    return pl.ds(pl.multiple_of(start, count), count)


def dot_last(a, b):
    return lax.dot_general(a, b, (((1,), (1,)), ((), ())), preferred_element_type=F32)


def dot_first(a, b):
    return lax.dot_general(a, b, (((0,), (0,)), ((), ())), preferred_element_type=F32)


def kernel(
    owner_ref,
    len_ref,
    q_hbm,
    k_hbm,
    v_hbm,
    cq_hbm,
    text_hbm,
    w_hbm,
    out_ref,
    slots,
    piece_out,
    pieces,
    sub_out,
    subs,
    sub_mine,
    prompt,
    weight,
    kv,
    queries,
    cross_q,
    parts,
    cross_kv,
    mixed,
    acc_out,
    accs,
    stat_out,
    stats,
    out_rows,
    ss,
    rs,
    kv_rs,
    acc_rs,
    stat_rs,
):
    me = lax.axis_index("seq")
    core = me % NC
    y = (me // NC) % NY
    z = (me // (NC * NY)) % NZ
    x = me // (NC * NY * NZ)
    f = x * NY + y
    xc = x * NC + core
    other = 1 - core

    local(text_hbm.at[0, rows(core * 64, 64), :], slots.at[core], rs.at[0])
    local(k_hbm.at[:, head_columns(z)], kv.at[y, 0, rows(z * TOK, TOK), :], rs.at[1])
    local(v_hbm.at[:, head_columns(z)], kv.at[y, 1, rows(z * TOK, TOK), :], rs.at[1])
    local(q_hbm.at[:, head_columns(z)], queries.at[xc, rows(z * TOK, TOK), :], rs.at[2])
    local(cq_hbm.at[:, head_columns(z)], cross_q.at[rows(z * TOK, TOK), :], rs.at[3])
    for j in range(2):
        local(w_hbm.at[:, head_columns(j * HEADS + z)], weight.at[j, z, core], rs.at[4])

    barrier = pltpu.get_barrier_semaphore()

    def greet(x, z, y, core):
        pl.semaphore_signal(
            barrier, inc=1, device_id={"seq": index_of(x, z, y, core)}, device_id_type=pl.DeviceIdType.MESH
        )

    def greet_line(t, carry):
        greet(x, (z + t) % NZ, y, core)
        return carry

    def greet_plane(t, carry):
        p = (f + t) % PLANE
        greet(p // NY, z, p % NY, core)
        return carry

    greet(x, z, y, other)
    greet(1 - x, z, y, other)
    lax.fori_loop(1, NZ, greet_line, 0)
    lax.fori_loop(1, PLANE, greet_plane, 0)
    pl.semaphore_wait(barrier, 2 + NZ - 1 + PLANE - 1)

    send(text_hbm.at[0, rows(other * 64, 64), :], slots.at[core], ss.at[0], rs.at[0], x, z, y, other)

    def line_kv(t, carry):
        zz = (z + t) % NZ
        send(k_hbm.at[:, head_columns(zz)], kv.at[y, 0, rows(z * TOK, TOK), :], ss.at[1], rs.at[1], x, zz, y, core)
        send(v_hbm.at[:, head_columns(zz)], kv.at[y, 1, rows(z * TOK, TOK), :], ss.at[1], rs.at[1], x, zz, y, core)
        return carry

    def line_q(t, carry):
        zz = (z + t) % NZ
        send(q_hbm.at[:, head_columns(zz)], queries.at[xc, rows(z * TOK, TOK), :], ss.at[2], rs.at[2], x, zz, y, core)
        return carry

    def line_cq(t, carry):
        zz = (z + t) % NZ
        send(cq_hbm.at[:, head_columns(zz)], cross_q.at[rows(z * TOK, TOK), :], ss.at[3], rs.at[3], x, zz, y, core)
        return carry

    def line_w(t, carry):
        zz = (z + t) % NZ
        for j in range(2):
            send(w_hbm.at[:, head_columns(j * HEADS + zz)], weight.at[j, z, core], ss.at[4], rs.at[4], x, zz, y, core)
        return carry

    lax.fori_loop(1, NZ, line_kv, 0)
    lax.fori_loop(1, NZ, line_q, 0)

    owner = owner_ref[0]
    owner_core = owner % NC
    wait_bytes(slots, rs.at[0])

    def cut_pair(pair):
        fx, yp = pair // 2, pair % 2
        for zp in range(NZ // 2):
            base = pl.multiple_of(fx * (NZ * 256) + yp * 128 + zp * 512, 128)
            a = slots[owner_core, :, pl.ds(base, 128)]
            b = slots[owner_core, :, pl.ds(pl.multiple_of(base + 256, 128), 128)]
            piece_out[pair * 2, :, zp * 128 : zp * 128 + 128] = jnp.concatenate([a[:, :64], b[:, :64]], axis=1)
            piece_out[pair * 2 + 1, :, zp * 128 : zp * 128 + 128] = jnp.concatenate([a[:, 64:], b[:, 64:]], axis=1)

    def send_piece(p):
        send(piece_out.at[p], pieces.at[f], ss.at[5], rs.at[5], p // NY, z, p % NY, core)

    def plane_pair(t, carry):
        pair = (f // 2 + t) % (PLANE // 2)
        cut_pair(pair)
        send_piece(pair * 2 + f % 2)
        send_piece(pair * 2 + 1 - f % 2)
        return carry

    lax.fori_loop(1, PLANE // 2, plane_pair, 0)
    cut_pair(f // 2)
    send_piece(f + 1 - 2 * (f % 2))
    local(piece_out.at[f], pieces.at[f], rs.at[5])

    lax.fori_loop(1, NZ, line_w, 0)
    lax.fori_loop(1, NZ, line_cq, 0)

    wait_bytes(kv.at[0], rs.at[1])
    for t in (2, 1, 3):
        send(kv.at[y], kv.at[y], ss.at[6], kv_rs.at[t - 1], x, z, (y + t) % NY, core)
    wait_bytes(queries.at[0], rs.at[2])
    for t in (2, 1, 3):
        p = (xc + t) % (NX * NC)
        send(queries.at[xc], queries.at[xc], ss.at[7], rs.at[6], p // NC, z, y, p % NC)

    wait_bytes(pieces, rs.at[5])
    piece = pieces[(owner // (NC * NY * NZ)) * NY + (owner // NC) % NY]
    for r in range(4):
        for c in range(2):
            sub_out[r * 2 + c] = piece[r * 16 : r * 16 + 16, c * 256 : c * 256 + 256]
    local(sub_out.at[z], subs.at[z], rs.at[7])

    def line_subs(t, carry):
        zz = (z + t) % NZ
        send(sub_out.at[zz], subs.at[z], ss.at[8], rs.at[7], x, zz, y, core)
        return carry

    lax.fori_loop(1, NZ, line_subs, 0)

    wait_bytes(weight.at[:, :, 0], rs.at[4])
    send(weight.at[:, :, core], weight.at[:, :, core], ss.at[14], rs.at[9], x, z, y, other)

    wait_bytes(subs, rs.at[7])
    sub_mine[...] = subs[(owner // (NC * NY)) % NZ]
    my_sub = prompt.at[z % 2, rows((z // 2) * 16, 16), :]
    local(sub_mine, my_sub, rs.at[8])

    def line_prompt(t, carry):
        send(sub_mine, my_sub, ss.at[11], rs.at[8], x, (z + t) % NZ, y, core)
        return carry

    lax.fori_loop(1, NZ, line_prompt, 0)

    for t in range(1, NY):
        wait_bytes(kv.at[0], kv_rs.at[t - 1])
    wait_bytes(queries.at[pl.ds(0, 3)], rs.at[6])

    def self_part(s):
        keys = kv[:, 0].reshape(NY * SLOT, HEAD_DIM)
        values = kv[:, 1].reshape(NY * SLOT, HEAD_DIM)
        scores = dot_last(keys, queries[s])
        top = jnp.max(scores, axis=0, keepdims=True)
        weights = jnp.exp2((scores - top) * SCALE)
        total = jnp.sum(weights, axis=0, keepdims=True)
        acc = dot_first(values, weights.astype(BF16)) * (1.0 / total)
        return acc.astype(BF16), top, total

    for t in (2, 1, 3):
        p = (xc + t) % (NX * NC)
        acc, top, total = self_part(p)
        acc_out[p] = acc
        stat_out[p, 0:1, :] = top
        stat_out[p, 1:2, :] = total
        send(acc_out.at[p], accs.at[xc], ss.at[9], acc_rs.at[t - 1], p // NC, z, y, p % NC)
        send(stat_out.at[p], stats.at[xc], ss.at[10], stat_rs.at[t - 1], p // NC, z, y, p % NC)

    wait_bytes(weight.at[:, :, 0], rs.at[9])
    wait_bytes(prompt, rs.at[8])
    for j in range(2):
        columns = weight[j].reshape(512, HEAD_DIM)
        part = jnp.dot(prompt[0], columns[:256], preferred_element_type=F32)
        part = part + jnp.dot(prompt[1], columns[256:], preferred_element_type=F32)
        parts[f, j] = part.astype(BF16)

    def plane_parts(t, carry):
        p = (f + t) % PLANE
        send(parts.at[f], parts.at[f], ss.at[12], rs.at[10], p // NY, z, p % NY, core)
        return carry

    lax.fori_loop(1, PLANE, plane_parts, 0)

    acc, top, total = self_part(xc)
    accs[xc] = acc
    stats[xc, 0:1, :] = top
    stats[xc, 1:2, :] = total

    for t in range(1, NX * NC):
        wait_bytes(accs.at[0], acc_rs.at[t - 1])
        wait_bytes(stats.at[0], stat_rs.at[t - 1])
    tops = [stats[s, 0:1, :] for s in range(NX * NC)]
    top = jnp.maximum(jnp.maximum(tops[0], tops[1]), jnp.maximum(tops[2], tops[3]))
    shares = [stats[s, 1:2, :] * jnp.exp2((tops[s] - top) * SCALE) for s in range(NX * NC)]
    whole = 1.0 / (shares[0] + shares[1] + shares[2] + shares[3])
    mixed[...] = sum(accs[s].astype(F32) * (shares[s] * whole) for s in range(NX * NC))

    wait_bytes(parts.at[pl.ds(0, 7)], rs.at[10])
    cross_kv[core] = jnp.sum(parts[...].astype(F32), axis=0).astype(BF16)
    send(cross_kv.at[core], cross_kv.at[core], ss.at[13], rs.at[12], x, z, y, other)

    wait_bytes(cross_q, rs.at[3])
    wait_bytes(cross_kv.at[0], rs.at[12])
    cross_keys = cross_kv[:, 0].reshape(NC * HALF, HEAD_DIM)
    cross_values = cross_kv[:, 1].reshape(NC * HALF, HEAD_DIM)
    scores = dot_last(cross_keys, cross_q[...])
    valid = lax.broadcasted_iota(jnp.int32, scores.shape, 0) < len_ref[0]
    scores = jnp.where(valid, scores, -1e30)
    weights = jnp.exp2((scores - jnp.max(scores, axis=0, keepdims=True)) * SCALE)
    total = jnp.sum(weights, axis=0, keepdims=True)
    result = mixed[...] + dot_first(cross_values, weights.astype(BF16)) * (1.0 / total)
    out_rows[...] = result.T.astype(BF16)

    local(out_rows.at[rows(z * TOK, TOK), :], out_ref.at[:, head_columns(z)], rs.at[11])

    def line_out(t, carry):
        zz = (z + t) % NZ
        send(out_rows.at[rows(zz * TOK, TOK), :], out_ref.at[:, head_columns(z)], ss.at[15], rs.at[11], x, zz, y, core)
        return carry

    lax.fori_loop(1, NZ, line_out, 0)

    wait_bytes(slots.at[0], ss.at[0])
    wait_bytes(kv.at[0, :, pl.ds(0, 224), :], ss.at[1])
    wait_bytes(queries.at[0, pl.ds(0, 224), :], ss.at[2])
    wait_bytes(queries.at[0, pl.ds(0, 224), :], ss.at[3])
    wait_bytes(kv.at[0, :, pl.ds(0, 224), :], ss.at[4])
    wait_bytes(pieces.at[pl.ds(0, 7)], ss.at[5])
    wait_bytes(kv.at[pl.ds(0, 3)], ss.at[6])
    wait_bytes(queries.at[pl.ds(0, 3)], ss.at[7])
    wait_bytes(subs.at[pl.ds(0, 7)], ss.at[8])
    wait_bytes(accs.at[pl.ds(0, 3)], ss.at[9])
    wait_bytes(stats.at[pl.ds(0, 3)], ss.at[10])
    wait_bytes(subs.at[pl.ds(0, 7)], ss.at[11])
    wait_bytes(parts.at[pl.ds(0, 7)], ss.at[12])
    wait_bytes(cross_kv.at[0], ss.at[13])
    wait_bytes(weight.at[:, :, 0], ss.at[14])
    wait_bytes(cross_q.at[pl.ds(0, 224), :], ss.at[15])
    wait_bytes(out_ref, rs.at[11])


def on_device(queries, keys, values, cross_queries, text_states, cross_kv_weight, owner, prompt_len):
    smem = pl.BlockSpec(memory_space=pltpu.SMEM)
    hbm = pl.BlockSpec(memory_space=pltpu.HBM)
    return pl.pallas_call(
        kernel,
        out_shape=jax.ShapeDtypeStruct((TOK, HEADS * HEAD_DIM), BF16),
        in_specs=[smem, smem] + [hbm] * 6,
        out_specs=pl.BlockSpec(memory_space=pltpu.VMEM),
        scratch_shapes=[
            pltpu.VMEM((NC, 64, 4096), BF16),
            pltpu.VMEM((PLANE, 64, 512), BF16),
            pltpu.VMEM((PLANE, 64, 512), BF16),
            pltpu.VMEM((NZ, 16, 256), BF16),
            pltpu.VMEM((NZ, 16, 256), BF16),
            pltpu.VMEM((16, 256), BF16),
            pltpu.VMEM((2, HALF, 256), BF16),
            pltpu.VMEM((2, NZ, NC, TOK, HEAD_DIM), BF16),
            pltpu.VMEM((NY, 2, SLOT, HEAD_DIM), BF16),
            pltpu.VMEM((NX * NC, SLOT, HEAD_DIM), BF16),
            pltpu.VMEM((SLOT, HEAD_DIM), BF16),
            pltpu.VMEM((PLANE, 2, HALF, HEAD_DIM), BF16),
            pltpu.VMEM((NC, 2, HALF, HEAD_DIM), BF16),
            pltpu.VMEM((HEAD_DIM, SLOT), F32),
            pltpu.VMEM((NX * NC, HEAD_DIM, SLOT), BF16),
            pltpu.VMEM((NX * NC, HEAD_DIM, SLOT), BF16),
            pltpu.VMEM((NX * NC, 8, SLOT), F32),
            pltpu.VMEM((NX * NC, 8, SLOT), F32),
            pltpu.VMEM((SLOT, HEAD_DIM), BF16),
            pltpu.SemaphoreType.DMA((16,)),
            pltpu.SemaphoreType.DMA((13,)),
            pltpu.SemaphoreType.DMA((NY - 1,)),
            pltpu.SemaphoreType.DMA((NX * NC - 1,)),
            pltpu.SemaphoreType.DMA((NX * NC - 1,)),
        ],
        compiler_params=pltpu.CompilerParams(
            collective_id=0, has_side_effects=True, vmem_limit_bytes=56 * 1024 * 1024
        ),
        cost_estimate=pl.CostEstimate(flops=700_000_000, bytes_accessed=2_000_000, transcendentals=1_100_000),
    )(owner, prompt_len, queries, keys, values, cross_queries, text_states, cross_kv_weight)


def solution(mesh):
    return jax.shard_map(
        on_device,
        mesh=mesh,
        in_specs=(
            P(("batch", "seq"), None),
            P(("batch", "seq"), None),
            P(("batch", "seq"), None),
            P(("batch", "seq"), None),
            P(("batch", "seq"), None, None),
            P("seq", None),
            P("batch"),
            P("batch"),
        ),
        out_specs=P(("batch", "seq"), None),
        check_vma=False,
    )
```

time: 50.6 us -> 45.4 us (0.90)
  Pallas kernels: 47.7 us -> 42.5 us
    pallas_call x1, Pallas kernels: 47.7 us -> 42.5 us  [on_device(): pl.pallas_call(kernel, out_shape=jax.ShapeDtypeStruct((TOK, HEADS * HEAD_...]
where the time goes in v2:
time: 45.4 us; the launch traced here: 45.3 us
  Pallas kernels  42.5 us (94%)
  local copies, waits for them, and re-layouts  1.47 us (3%)
  between operations  1.3 us (3%)
    pallas_call x1, Pallas kernels, on_device(): pl.pallas_call(kernel, out_shape=jax.ShapeDtypeStruct((TOK, HEADS * HEAD_...  42.5 us
    unnamed x1, local copies, waits for them, and re-layouts  1.47 us

profile of v2, /device:TPU:1, one launch (start us, length us, event | category | flops | bytes accessed | tf_op | source)
XLA Modules:
  0.0 45.3 jit_solution(2343557156903309704)
XLA Ops:
  1.3 42.5 %shard_map.82 = bf16[32,1024]{1,0:T(8,128)(2,1)} custom-call(s32[1]{0:T(128)S(6)} %copy.10.owner_ref, s32[1]{0:T(128)S(6)} %copy.11.len_ref, bf16[32,1024]{1,0:T(8,128)(2,1)} %q_hbm.1, bf16[32,1024]{1,0:T(8,128)(2,1)} %k_hbm.1, bf16[32,1024]{1,0:T(8,128)(2,1)} %v_hbm.1, bf16[32,1024]{1,0:T(8,128)(2,1)} %cq_hbm.1, bf16[1,128,4096]{2,1,0:T(8,128)(2,1)} %text_hbm.1, ...), custom_call_target="tpu_custom_call" | custom-call | flops 700000000 | bytes 2000000 | tf_op jit(solution)/shard_map/pallas_call | solution.py:328
  43.8 1.5 %copy.12 = bf16[32,1024]{1,0:T(8,128)(2,1)} copy(bf16[32,1024]{1,0:T(8,128)(2,1)} %shard_map.82) | data formatting | bytes 131072

commit v3 on v2

--- a/solution.py
+++ b/solution.py
@@ -15,6 +15,8 @@
 SLOT = TOK * NZ
 SCALE = math.log2(math.e) / math.sqrt(HEAD_DIM)
 HALF = 64
+LINE = (4, 3, 5, 2, 6, 1, 7)
+ACROSS = (6, 5, 7, 2, 4, 1, 3)
 F32 = jnp.float32
 BF16 = jnp.bfloat16
 
@@ -32,6 +34,11 @@
         device_id={"seq": index_of(x, z, y, core)},
         device_id_type=pl.DeviceIdType.MESH,
     ).start()
+
+
+def each(steps, fn):
+    for t in steps:
+        fn(t)
 
 
 def local(src, dst, sem):
@@ -79,6 +86,7 @@
     kv,
     queries,
     cross_q,
+    part_out,
     parts,
     cross_kv,
     mixed,
@@ -92,6 +100,7 @@
     kv_rs,
     acc_rs,
     stat_rs,
+    vouch,
 ):
     me = lax.axis_index("seq")
     core = me % NC
@@ -112,52 +121,50 @@
 
     barrier = pltpu.get_barrier_semaphore()
 
-    def greet(x, z, y, core):
+    def greet(sem, x, z, y, core):
         pl.semaphore_signal(
-            barrier, inc=1, device_id={"seq": index_of(x, z, y, core)}, device_id_type=pl.DeviceIdType.MESH
+            sem, inc=1, device_id={"seq": index_of(x, z, y, core)}, device_id_type=pl.DeviceIdType.MESH
         )
 
-    def greet_line(t, carry):
-        greet(x, (z + t) % NZ, y, core)
-        return carry
-
-    def greet_plane(t, carry):
-        p = (f + t) % PLANE
-        greet(p // NY, z, p % NY, core)
-        return carry
-
-    greet(x, z, y, other)
-    greet(1 - x, z, y, other)
-    lax.fori_loop(1, NZ, greet_line, 0)
-    lax.fori_loop(1, PLANE, greet_plane, 0)
-    pl.semaphore_wait(barrier, 2 + NZ - 1 + PLANE - 1)
+    for t in (2, 6):
+        greet(barrier, x, (z + t) % NZ, y, core)
+    for t in (2, 1, 3):
+        greet(barrier, x, z, (y + t) % NY, core)
+    for t in (1, 7):
+        greet(barrier, x, (z + t) % NZ, y, core)
+    greet(barrier, 1 - x, z, y, core)
+    greet(barrier, x, z, y, other)
+    pl.semaphore_wait(barrier, 9)
 
     send(text_hbm.at[0, rows(other * 64, 64), :], slots.at[core], ss.at[0], rs.at[0], x, z, y, other)
 
-    def line_kv(t, carry):
+    greet(vouch.at[0], 1 - x, z, y, core)
+    for t in (2, 6):
+        greet(vouch.at[1], x, (z + t) % NZ, y, core)
+
+    def line_kv(t):
         zz = (z + t) % NZ
         send(k_hbm.at[:, head_columns(zz)], kv.at[y, 0, rows(z * TOK, TOK), :], ss.at[1], rs.at[1], x, zz, y, core)
         send(v_hbm.at[:, head_columns(zz)], kv.at[y, 1, rows(z * TOK, TOK), :], ss.at[1], rs.at[1], x, zz, y, core)
-        return carry
-
-    def line_q(t, carry):
+
+    def line_q(t):
         zz = (z + t) % NZ
         send(q_hbm.at[:, head_columns(zz)], queries.at[xc, rows(z * TOK, TOK), :], ss.at[2], rs.at[2], x, zz, y, core)
-        return carry
-
-    def line_cq(t, carry):
+
+    def line_cq(t):
         zz = (z + t) % NZ
         send(cq_hbm.at[:, head_columns(zz)], cross_q.at[rows(z * TOK, TOK), :], ss.at[3], rs.at[3], x, zz, y, core)
-        return carry
-
-    def line_w(t, carry):
+
+    def line_w(t):
         zz = (z + t) % NZ
         for j in range(2):
             send(w_hbm.at[:, head_columns(j * HEADS + zz)], weight.at[j, z, core], ss.at[4], rs.at[4], x, zz, y, core)
-        return carry
-
-    lax.fori_loop(1, NZ, line_kv, 0)
-    lax.fori_loop(1, NZ, line_q, 0)
+
+    each((2, 6, 1, 7), line_kv)
+    pl.semaphore_wait(vouch.at[0], 1)
+    pl.semaphore_wait(vouch.at[1], 2)
+    each((4, 3, 5), line_kv)
+    each(LINE, line_q)
 
     owner = owner_ref[0]
     owner_core = owner % NC
@@ -187,8 +194,8 @@
     send_piece(f + 1 - 2 * (f % 2))
     local(piece_out.at[f], pieces.at[f], rs.at[5])
 
-    lax.fori_loop(1, NZ, line_w, 0)
-    lax.fori_loop(1, NZ, line_cq, 0)
+    each(LINE, line_w)
+    each(LINE, line_cq)
 
     wait_bytes(kv.at[0], rs.at[1])
     for t in (2, 1, 3):
@@ -205,12 +212,11 @@
             sub_out[r * 2 + c] = piece[r * 16 : r * 16 + 16, c * 256 : c * 256 + 256]
     local(sub_out.at[z], subs.at[z], rs.at[7])
 
-    def line_subs(t, carry):
+    def line_subs(t):
         zz = (z + t) % NZ
         send(sub_out.at[zz], subs.at[z], ss.at[8], rs.at[7], x, zz, y, core)
-        return carry
-
-    lax.fori_loop(1, NZ, line_subs, 0)
+
+    each(LINE, line_subs)
 
     wait_bytes(weight.at[:, :, 0], rs.at[4])
     send(weight.at[:, :, core], weight.at[:, :, core], ss.at[14], rs.at[9], x, z, y, other)
@@ -220,11 +226,10 @@
     my_sub = prompt.at[z % 2, rows((z // 2) * 16, 16), :]
     local(sub_mine, my_sub, rs.at[8])
 
-    def line_prompt(t, carry):
+    def line_prompt(t):
         send(sub_mine, my_sub, ss.at[11], rs.at[8], x, (z + t) % NZ, y, core)
-        return carry
-
-    lax.fori_loop(1, NZ, line_prompt, 0)
+
+    each(LINE, line_prompt)
 
     for t in range(1, NY):
         wait_bytes(kv.at[0], kv_rs.at[t - 1])
@@ -255,19 +260,32 @@
         columns = weight[j].reshape(512, HEAD_DIM)
         part = jnp.dot(prompt[0], columns[:256], preferred_element_type=F32)
         part = part + jnp.dot(prompt[1], columns[256:], preferred_element_type=F32)
-        parts[f, j] = part.astype(BF16)
-
-    def plane_parts(t, carry):
-        p = (f + t) % PLANE
-        send(parts.at[f], parts.at[f], ss.at[12], rs.at[10], p // NY, z, p % NY, core)
-        return carry
-
-    lax.fori_loop(1, PLANE, plane_parts, 0)
+        part_out[:, j] = part.reshape(PLANE, 8, HEAD_DIM)
+
+    def plane_parts(t):
+        px, py = (x + t // NY) % NX, (y + t) % NY
+        p = px * NY + py
+        send(part_out.at[p], parts.at[f], ss.at[12], rs.at[10], px, z, py, core)
+
+    each(ACROSS, plane_parts)
+    parts[f] = part_out[f]
 
     acc, top, total = self_part(xc)
     accs[xc] = acc
     stats[xc, 0:1, :] = top
     stats[xc, 1:2, :] = total
+
+    wait_bytes(parts.at[pl.ds(0, 7)], rs.at[10])
+    cross_kv[core, f] = jnp.sum(parts[...], axis=0).reshape(16, HEAD_DIM).astype(BF16)
+
+    def plane_rows(t):
+        px, py = (x + t // NY) % NX, (y + t) % NY
+        p = px * NY + py
+        for c in (core, other):
+            send(cross_kv.at[core, f], cross_kv.at[core, f], ss.at[13], rs.at[12], px, z, py, c)
+
+    each(ACROSS, plane_rows)
+    send(cross_kv.at[core, f], cross_kv.at[core, f], ss.at[13], rs.at[12], x, z, y, other)
 
     for t in range(1, NX * NC):
         wait_bytes(accs.at[0], acc_rs.at[t - 1])
@@ -278,14 +296,11 @@
     whole = 1.0 / (shares[0] + shares[1] + shares[2] + shares[3])
     mixed[...] = sum(accs[s].astype(F32) * (shares[s] * whole) for s in range(NX * NC))
 
-    wait_bytes(parts.at[pl.ds(0, 7)], rs.at[10])
-    cross_kv[core] = jnp.sum(parts[...].astype(F32), axis=0).astype(BF16)
-    send(cross_kv.at[core], cross_kv.at[core], ss.at[13], rs.at[12], x, z, y, other)
-
     wait_bytes(cross_q, rs.at[3])
-    wait_bytes(cross_kv.at[0], rs.at[12])
-    cross_keys = cross_kv[:, 0].reshape(NC * HALF, HEAD_DIM)
-    cross_values = cross_kv[:, 1].reshape(NC * HALF, HEAD_DIM)
+    wait_bytes(cross_q.at[pl.ds(0, 240), :], rs.at[12])
+    cross = cross_kv[...].astype(F32)
+    cross_keys = cross[:, :, :8].reshape(NC * HALF, HEAD_DIM).astype(BF16)
+    cross_values = cross[:, :, 8:].reshape(NC * HALF, HEAD_DIM).astype(BF16)
     scores = dot_last(cross_keys, cross_q[...])
     valid = lax.broadcasted_iota(jnp.int32, scores.shape, 0) < len_ref[0]
     scores = jnp.where(valid, scores, -1e30)
@@ -296,12 +311,11 @@
 
     local(out_rows.at[rows(z * TOK, TOK), :], out_ref.at[:, head_columns(z)], rs.at[11])
 
-    def line_out(t, carry):
+    def line_out(t):
         zz = (z + t) % NZ
         send(out_rows.at[rows(zz * TOK, TOK), :], out_ref.at[:, head_columns(z)], ss.at[15], rs.at[11], x, zz, y, core)
-        return carry
-
-    lax.fori_loop(1, NZ, line_out, 0)
+
+    each(LINE, line_out)
 
     wait_bytes(slots.at[0], ss.at[0])
     wait_bytes(kv.at[0, :, pl.ds(0, 224), :], ss.at[1])
@@ -316,7 +330,7 @@
     wait_bytes(stats.at[pl.ds(0, 3)], ss.at[10])
     wait_bytes(subs.at[pl.ds(0, 7)], ss.at[11])
     wait_bytes(parts.at[pl.ds(0, 7)], ss.at[12])
-    wait_bytes(cross_kv.at[0], ss.at[13])
+    wait_bytes(cross_q.at[pl.ds(0, 240), :], ss.at[13])
     wait_bytes(weight.at[:, :, 0], ss.at[14])
     wait_bytes(cross_q.at[pl.ds(0, 224), :], ss.at[15])
     wait_bytes(out_ref, rs.at[11])
@@ -327,7 +341,7 @@
     hbm = pl.BlockSpec(memory_space=pltpu.HBM)
     return pl.pallas_call(
         kernel,
-        out_shape=jax.ShapeDtypeStruct((TOK, HEADS * HEAD_DIM), BF16),
+        out_shape=pltpu.VMEM((TOK, HEADS * HEAD_DIM), BF16),
         in_specs=[smem, smem] + [hbm] * 6,
         out_specs=pl.BlockSpec(memory_space=pltpu.VMEM),
         scratch_shapes=[
@@ -342,8 +356,9 @@
             pltpu.VMEM((NY, 2, SLOT, HEAD_DIM), BF16),
             pltpu.VMEM((NX * NC, SLOT, HEAD_DIM), BF16),
             pltpu.VMEM((SLOT, HEAD_DIM), BF16),
-            pltpu.VMEM((PLANE, 2, HALF, HEAD_DIM), BF16),
-            pltpu.VMEM((NC, 2, HALF, HEAD_DIM), BF16),
+            pltpu.VMEM((PLANE, 2, 8, HEAD_DIM), F32),
+            pltpu.VMEM((PLANE, 2, 8, HEAD_DIM), F32),
+            pltpu.VMEM((NC, PLANE, 16, HEAD_DIM), BF16),
             pltpu.VMEM((HEAD_DIM, SLOT), F32),
             pltpu.VMEM((NX * NC, HEAD_DIM, SLOT), BF16),
             pltpu.VMEM((NX * NC, HEAD_DIM, SLOT), BF16),
@@ -355,6 +370,7 @@
             pltpu.SemaphoreType.DMA((NY - 1,)),
             pltpu.SemaphoreType.DMA((NX * NC - 1,)),
             pltpu.SemaphoreType.DMA((NX * NC - 1,)),
+            pltpu.SemaphoreType.REGULAR((2,)),
         ],
         compiler_params=pltpu.CompilerParams(
             collective_id=0, has_side_effects=True, vmem_limit_bytes=56 * 1024 * 1024

time: 45.4 us -> 44.9 us (0.989)
  local copies, waits for them, and re-layouts: 1.47 us -> 0.63 us
    unnamed x1, local copies, waits for them, and re-layouts: 1.47 us -> 0.63 us
where the time goes in v3:
time: 44.9 us; the launch traced here: 44.8 us
  Pallas kernels  42.9 us (96%)
  between operations  1.3 us (3%)
  local copies, waits for them, and re-layouts  0.63 us (1%)
    pallas_call x1, Pallas kernels, on_device(): pl.pallas_call(kernel, out_shape=pltpu.VMEM((TOK, HEADS * HEAD_DIM), BF16...  42.9 us

profile of v3, /device:TPU:1, one launch (start us, length us, event | category | flops | bytes accessed | tf_op | source)
XLA Modules:
  0.0 44.8 jit_solution(3944111188028300737)
XLA Ops:
  1.3 42.9 %shard_map.82 = bf16[32,1024]{1,0:T(8,128)(2,1)S(1)} custom-call(s32[1]{0:T(128)S(6)} %copy.11.owner_ref, s32[1]{0:T(128)S(6)} %copy.12.len_ref, bf16[32,1024]{1,0:T(8,128)(2,1)} %q_hbm.1, bf16[32,1024]{1,0:T(8,128)(2,1)} %k_hbm.1, bf16[32,1024]{1,0:T(8,128)(2,1)} %v_hbm.1, bf16[32,1024]{1,0:T(8,128)(2,1)} %cq_hbm.1, bf16[1,128,4096]{2,1,0:T(8,128)(2,1)} %text_hbm.1, ...), custom_call_target="tpu_custom_call" | custom-call | flops 700000000 | bytes 2000000 | tf_op jit(solution)/shard_map/pallas_call | solution.py:342
  44.2 0.6 %copy.10 = bf16[32,1024]{1,0:T(8,128)(2,1)} copy(bf16[32,1024]{1,0:T(8,128)(2,1)S(1)} %shard_map.82) | data formatting | bytes 131072

commit v4 on v3

--- a/solution.py
+++ b/solution.py
@@ -53,6 +53,10 @@
     return pl.ds(pl.multiple_of(head * HEAD_DIM, HEAD_DIM), HEAD_DIM)
 
 
+def half(x, i):
+    return pl.ds(pl.multiple_of((x + 1 - i) % NX * 2048, 2048), 2048)
+
+
 def rows(start, count):
     return pl.ds(pl.multiple_of(start, count), count)
 
@@ -75,7 +79,8 @@
     text_hbm,
     w_hbm,
     out_ref,
-    slots,
+    slots_far,
+    slots_near,
     piece_out,
     pieces,
     sub_out,
@@ -101,6 +106,7 @@
     acc_rs,
     stat_rs,
     vouch,
+    halves,
 ):
     me = lax.axis_index("seq")
     core = me % NC
@@ -110,8 +116,39 @@
     f = x * NY + y
     xc = x * NC + core
     other = 1 - core
-
-    local(text_hbm.at[0, rows(core * 64, 64), :], slots.at[core], rs.at[0])
+    halves_of = (slots_far, slots_near)
+
+    barrier = pltpu.get_barrier_semaphore()
+
+    def greet(sem, x, z, y, core):
+        pl.semaphore_signal(
+            sem, inc=1, device_id={"seq": index_of(x, z, y, core)}, device_id_type=pl.DeviceIdType.MESH
+        )
+
+    for t in (1, 7):
+        greet(barrier, x, (z + t) % NZ, y, core)
+    for t in (1, 3):
+        greet(barrier, x, z, (y + t) % NY, core)
+    greet(barrier, 1 - x, z, y, core)
+    greet(barrier, x, z, y, other)
+    for i in range(NX):
+        local(text_hbm.at[0, rows(core * 64, 64), half(x, i)], halves_of[i].at[core], halves.at[i])
+    pl.semaphore_wait(barrier, 6)
+
+    theirs = rows(other * 64, 64)
+    for i in range(NX):
+        columns = half(x, i)
+        send(text_hbm.at[0, theirs, columns], halves_of[i].at[core], ss.at[0], halves.at[i], x, z, y, other)
+
+    def vouch_to(i, steps_y, steps_z):
+        for t in steps_y:
+            greet(vouch.at[i], x, z, (y + t) % NY, core)
+        for t in steps_z:
+            greet(vouch.at[i], x, (z + t) % NZ, y, core)
+
+    vouch_to(0, (1, 3), ())
+    vouch_to(1, (), (1, 7))
+
     local(k_hbm.at[:, head_columns(z)], kv.at[y, 0, rows(z * TOK, TOK), :], rs.at[1])
     local(v_hbm.at[:, head_columns(z)], kv.at[y, 1, rows(z * TOK, TOK), :], rs.at[1])
     local(q_hbm.at[:, head_columns(z)], queries.at[xc, rows(z * TOK, TOK), :], rs.at[2])
@@ -119,29 +156,6 @@
     for j in range(2):
         local(w_hbm.at[:, head_columns(j * HEADS + z)], weight.at[j, z, core], rs.at[4])
 
-    barrier = pltpu.get_barrier_semaphore()
-
-    def greet(sem, x, z, y, core):
-        pl.semaphore_signal(
-            sem, inc=1, device_id={"seq": index_of(x, z, y, core)}, device_id_type=pl.DeviceIdType.MESH
-        )
-
-    for t in (2, 6):
-        greet(barrier, x, (z + t) % NZ, y, core)
-    for t in (2, 1, 3):
-        greet(barrier, x, z, (y + t) % NY, core)
-    for t in (1, 7):
-        greet(barrier, x, (z + t) % NZ, y, core)
-    greet(barrier, 1 - x, z, y, core)
-    greet(barrier, x, z, y, other)
-    pl.semaphore_wait(barrier, 9)
-
-    send(text_hbm.at[0, rows(other * 64, 64), :], slots.at[core], ss.at[0], rs.at[0], x, z, y, other)
-
-    greet(vouch.at[0], 1 - x, z, y, core)
-    for t in (2, 6):
-        greet(vouch.at[1], x, (z + t) % NZ, y, core)
-
     def line_kv(t):
         zz = (z + t) % NZ
         send(k_hbm.at[:, head_columns(zz)], kv.at[y, 0, rows(z * TOK, TOK), :], ss.at[1], rs.at[1], x, zz, y, core)
@@ -160,20 +174,22 @@
         for j in range(2):
             send(w_hbm.at[:, head_columns(j * HEADS + zz)], weight.at[j, z, core], ss.at[4], rs.at[4], x, zz, y, core)
 
-    each((2, 6, 1, 7), line_kv)
-    pl.semaphore_wait(vouch.at[0], 1)
+    each((1, 7), line_kv)
+    each((1, 7), line_q)
+    pl.semaphore_wait(vouch.at[0], 2)
+    greet(vouch.at[4], 1 - x, z, y, core)
     pl.semaphore_wait(vouch.at[1], 2)
-    each((4, 3, 5), line_kv)
-    each(LINE, line_q)
+    vouch_to(2, (), (1, 7))
+    each((2, 6), line_kv)
+    each((2, 6), line_q)
 
     owner = owner_ref[0]
     owner_core = owner % NC
-    wait_bytes(slots, rs.at[0])
-
-    def cut_pair(pair):
-        fx, yp = pair // 2, pair % 2
+    wait_bytes(slots_far, halves.at[0])
+
+    def cut_pair(slots, pair):
         for zp in range(NZ // 2):
-            base = pl.multiple_of(fx * (NZ * 256) + yp * 128 + zp * 512, 128)
+            base = pl.multiple_of(pair % 2 * 128 + zp * 512, 128)
             a = slots[owner_core, :, pl.ds(base, 128)]
             b = slots[owner_core, :, pl.ds(pl.multiple_of(base + 256, 128), 128)]
             piece_out[pair * 2, :, zp * 128 : zp * 128 + 128] = jnp.concatenate([a[:, :64], b[:, :64]], axis=1)
@@ -182,18 +198,25 @@
     def send_piece(p):
         send(piece_out.at[p], pieces.at[f], ss.at[5], rs.at[5], p // NY, z, p % NY, core)
 
-    def plane_pair(t, carry):
-        pair = (f // 2 + t) % (PLANE // 2)
-        cut_pair(pair)
-        send_piece(pair * 2 + f % 2)
-        send_piece(pair * 2 + 1 - f % 2)
-        return carry
-
-    lax.fori_loop(1, PLANE // 2, plane_pair, 0)
-    cut_pair(f // 2)
-    send_piece(f + 1 - 2 * (f % 2))
+    for i in range(NX):
+        if i == 1:
+            wait_bytes(slots_near, halves.at[1])
+        px = (x + 1 - i) % NX
+        for j in range(2):
+            cut_pair(halves_of[i], px * 2 + j)
+        for step in ((1, 3, 0), (2, 1, 3))[i]:
+            send_piece(px * NY + (y + step) % NY)
     local(piece_out.at[f], pieces.at[f], rs.at[5])
 
+    pl.semaphore_wait(vouch.at[2], 2)
+    vouch_to(3, (), (1, 7))
+    pl.semaphore_wait(vouch.at[4], 1)
+    send_piece((1 - x) * NY + (y + 2) % NY)
+    each((3, 5), line_kv)
+    each((3, 5), line_q)
+    pl.semaphore_wait(vouch.at[3], 2)
+    each((4,), line_kv)
+    each((4,), line_q)
     each(LINE, line_w)
     each(LINE, line_cq)
 
@@ -210,13 +233,13 @@
     for r in range(4):
         for c in range(2):
             sub_out[r * 2 + c] = piece[r * 16 : r * 16 + 16, c * 256 : c * 256 + 256]
+
+    def line_subs(t):
+        zz = (z + t) % NZ
+        send(sub_out.at[zz], subs.at[z], ss.at[8], rs.at[7], x, zz, y, core)
+
+    each(LINE, line_subs)
     local(sub_out.at[z], subs.at[z], rs.at[7])
-
-    def line_subs(t):
-        zz = (z + t) % NZ
-        send(sub_out.at[zz], subs.at[z], ss.at[8], rs.at[7], x, zz, y, core)
-
-    each(LINE, line_subs)
 
     wait_bytes(weight.at[:, :, 0], rs.at[4])
     send(weight.at[:, :, core], weight.at[:, :, core], ss.at[14], rs.at[9], x, z, y, other)
@@ -224,12 +247,12 @@
     wait_bytes(subs, rs.at[7])
     sub_mine[...] = subs[(owner // (NC * NY)) % NZ]
     my_sub = prompt.at[z % 2, rows((z // 2) * 16, 16), :]
-    local(sub_mine, my_sub, rs.at[8])
 
     def line_prompt(t):
         send(sub_mine, my_sub, ss.at[11], rs.at[8], x, (z + t) % NZ, y, core)
 
     each(LINE, line_prompt)
+    local(sub_mine, my_sub, rs.at[8])
 
     for t in range(1, NY):
         wait_bytes(kv.at[0], kv_rs.at[t - 1])
@@ -309,15 +332,15 @@
     result = mixed[...] + dot_first(cross_values, weights.astype(BF16)) * (1.0 / total)
     out_rows[...] = result.T.astype(BF16)
 
+
+    def line_out(t):
+        zz = (z + t) % NZ
+        send(out_rows.at[rows(zz * TOK, TOK), :], out_ref.at[:, head_columns(z)], ss.at[15], rs.at[11], x, zz, y, core)
+
+    each(LINE, line_out)
     local(out_rows.at[rows(z * TOK, TOK), :], out_ref.at[:, head_columns(z)], rs.at[11])
 
-    def line_out(t):
-        zz = (z + t) % NZ
-        send(out_rows.at[rows(zz * TOK, TOK), :], out_ref.at[:, head_columns(z)], ss.at[15], rs.at[11], x, zz, y, core)
-
-    each(LINE, line_out)
-
-    wait_bytes(slots.at[0], ss.at[0])
+    wait_bytes(slots_far, ss.at[0])
     wait_bytes(kv.at[0, :, pl.ds(0, 224), :], ss.at[1])
     wait_bytes(queries.at[0, pl.ds(0, 224), :], ss.at[2])
     wait_bytes(queries.at[0, pl.ds(0, 224), :], ss.at[3])
@@ -345,7 +368,8 @@
         in_specs=[smem, smem] + [hbm] * 6,
         out_specs=pl.BlockSpec(memory_space=pltpu.VMEM),
         scratch_shapes=[
-            pltpu.VMEM((NC, 64, 4096), BF16),
+            pltpu.VMEM((NC, 64, 2048), BF16),
+            pltpu.VMEM((NC, 64, 2048), BF16),
             pltpu.VMEM((PLANE, 64, 512), BF16),
             pltpu.VMEM((PLANE, 64, 512), BF16),
             pltpu.VMEM((NZ, 16, 256), BF16),
@@ -370,7 +394,8 @@
             pltpu.SemaphoreType.DMA((NY - 1,)),
             pltpu.SemaphoreType.DMA((NX * NC - 1,)),
             pltpu.SemaphoreType.DMA((NX * NC - 1,)),
-            pltpu.SemaphoreType.REGULAR((2,)),
+            pltpu.SemaphoreType.REGULAR((5,)),
+            pltpu.SemaphoreType.DMA((NX,)),
         ],
         compiler_params=pltpu.CompilerParams(
             collective_id=0, has_side_effects=True, vmem_limit_bytes=56 * 1024 * 1024

time: 44.9 us -> 43.8 us (0.976)
  Pallas kernels: 42.9 us -> 41.8 us
    pallas_call x1, Pallas kernels: 42.9 us -> 41.8 us  [on_device(): pl.pallas_call(kernel, out_shape=pltpu.VMEM((TOK, HEADS * HEAD_DIM), BF16...]
where the time goes in v4:
time: 43.8 us
  Pallas kernels  41.8 us (95%)
  between operations  1.3 us (3%)
  local copies, waits for them, and re-layouts  0.63 us (1%)
    pallas_call x1, Pallas kernels, on_device(): pl.pallas_call(kernel, out_shape=pltpu.VMEM((TOK, HEADS * HEAD_DIM), BF16...  41.8 us

profile of v4, /device:TPU:1, one launch (start us, length us, event | category | flops | bytes accessed | tf_op | source)
XLA Modules:
  0.0 43.8 jit_solution(14990774617316609427)
XLA Ops:
  1.3 41.8 %shard_map.82 = bf16[32,1024]{1,0:T(8,128)(2,1)S(1)} custom-call(s32[1]{0:T(128)S(6)} %copy.11.owner_ref, s32[1]{0:T(128)S(6)} %copy.12.len_ref, bf16[32,1024]{1,0:T(8,128)(2,1)} %q_hbm.1, bf16[32,1024]{1,0:T(8,128)(2,1)} %k_hbm.1, bf16[32,1024]{1,0:T(8,128)(2,1)} %v_hbm.1, bf16[32,1024]{1,0:T(8,128)(2,1)} %cq_hbm.1, bf16[1,128,4096]{2,1,0:T(8,128)(2,1)} %text_hbm.1, ...), custom_call_target="tpu_custom_call" | custom-call | flops 700000000 | bytes 2000000 | tf_op jit(solution)/shard_map/pallas_call | solution.py:365
  43.1 0.6 %copy.10 = bf16[32,1024]{1,0:T(8,128)(2,1)} copy(bf16[32,1024]{1,0:T(8,128)(2,1)S(1)} %shard_map.82) | data formatting | bytes 131072

commit v5 on v4

--- a/solution.py
+++ b/solution.py
@@ -54,7 +54,7 @@
 
 
 def half(x, i):
-    return pl.ds(pl.multiple_of((x + 1 - i) % NX * 2048, 2048), 2048)
+    return pl.ds(pl.multiple_of((x + i) % NX * 2048, 2048), 2048)
 
 
 def rows(start, count):
@@ -79,8 +79,8 @@
     text_hbm,
     w_hbm,
     out_ref,
-    slots_far,
-    slots_near,
+    slots_a,
+    slots_b,
     piece_out,
     pieces,
     sub_out,
@@ -116,7 +116,7 @@
     f = x * NY + y
     xc = x * NC + core
     other = 1 - core
-    halves_of = (slots_far, slots_near)
+    halves_of = (slots_a, slots_b)
 
     barrier = pltpu.get_barrier_semaphore()
 
@@ -125,29 +125,34 @@
             sem, inc=1, device_id={"seq": index_of(x, z, y, core)}, device_id_type=pl.DeviceIdType.MESH
         )
 
-    for t in (1, 7):
-        greet(barrier, x, (z + t) % NZ, y, core)
-    for t in (1, 3):
-        greet(barrier, x, z, (y + t) % NY, core)
-    greet(barrier, 1 - x, z, y, core)
+    for t in (2, 6, 1, 7):
+        greet(barrier, x, (z + t) % NZ, y, 1)
+    for t in (2, 1, 3):
+        greet(barrier, x, z, (y + t) % NY, 1)
+    greet(barrier, 1 - x, z, y, 1)
     greet(barrier, x, z, y, other)
     for i in range(NX):
         local(text_hbm.at[0, rows(core * 64, 64), half(x, i)], halves_of[i].at[core], halves.at[i])
-    pl.semaphore_wait(barrier, 6)
+
+    @pl.when(core == 0)
+    def _():
+        pl.semaphore_wait(barrier, 1)
+
+    @pl.when(core == 1)
+    def _():
+        pl.semaphore_wait(barrier, 17)
 
     theirs = rows(other * 64, 64)
     for i in range(NX):
         columns = half(x, i)
         send(text_hbm.at[0, theirs, columns], halves_of[i].at[core], ss.at[0], halves.at[i], x, z, y, other)
 
-    def vouch_to(i, steps_y, steps_z):
-        for t in steps_y:
-            greet(vouch.at[i], x, z, (y + t) % NY, core)
-        for t in steps_z:
-            greet(vouch.at[i], x, (z + t) % NZ, y, core)
-
-    vouch_to(0, (1, 3), ())
-    vouch_to(1, (), (1, 7))
+    @pl.when(core == 1)
+    def _():
+        greet(vouch.at[0], x, z, y, 0)
+        greet(vouch.at[1], 1 - x, z, y, 1)
+        for t in (2, 6):
+            greet(vouch.at[2], x, (z + t) % NZ, y, 1)
 
     local(k_hbm.at[:, head_columns(z)], kv.at[y, 0, rows(z * TOK, TOK), :], rs.at[1])
     local(v_hbm.at[:, head_columns(z)], kv.at[y, 1, rows(z * TOK, TOK), :], rs.at[1])
@@ -174,18 +179,13 @@
         for j in range(2):
             send(w_hbm.at[:, head_columns(j * HEADS + zz)], weight.at[j, z, core], ss.at[4], rs.at[4], x, zz, y, core)
 
-    each((1, 7), line_kv)
-    each((1, 7), line_q)
-    pl.semaphore_wait(vouch.at[0], 2)
-    greet(vouch.at[4], 1 - x, z, y, core)
-    pl.semaphore_wait(vouch.at[1], 2)
-    vouch_to(2, (), (1, 7))
-    each((2, 6), line_kv)
-    each((2, 6), line_q)
+    @pl.when(core == 0)
+    def _():
+        pl.semaphore_wait(vouch.at[0], 1)
 
     owner = owner_ref[0]
     owner_core = owner % NC
-    wait_bytes(slots_far, halves.at[0])
+    wait_bytes(slots_a, halves.at[0])
 
     def cut_pair(slots, pair):
         for zp in range(NZ // 2):
@@ -200,23 +200,39 @@
 
     for i in range(NX):
         if i == 1:
-            wait_bytes(slots_near, halves.at[1])
-        px = (x + 1 - i) % NX
+            wait_bytes(slots_b, halves.at[1])
+        px = (x + i) % NX
         for j in range(2):
             cut_pair(halves_of[i], px * 2 + j)
-        for step in ((1, 3, 0), (2, 1, 3))[i]:
+        for step in ((2, 1, 3), (0,))[i]:
             send_piece(px * NY + (y + step) % NY)
     local(piece_out.at[f], pieces.at[f], rs.at[5])
 
-    pl.semaphore_wait(vouch.at[2], 2)
-    vouch_to(3, (), (1, 7))
-    pl.semaphore_wait(vouch.at[4], 1)
-    send_piece((1 - x) * NY + (y + 2) % NY)
-    each((3, 5), line_kv)
-    each((3, 5), line_q)
-    pl.semaphore_wait(vouch.at[3], 2)
-    each((4,), line_kv)
-    each((4,), line_q)
+    each((2, 6, 1, 7), line_kv)
+
+    @pl.when(core == 1)
+    def _():
+        pl.semaphore_wait(vouch.at[1], 1)
+        greet(vouch.at[3], x, z, y, 0)
+
+    @pl.when(core == 0)
+    def _():
+        pl.semaphore_wait(vouch.at[3], 1)
+
+    for step in (2, 1, 3):
+        send_piece((1 - x) * NY + (y + step) % NY)
+
+    @pl.when(core == 1)
+    def _():
+        pl.semaphore_wait(vouch.at[2], 2)
+        greet(vouch.at[4], x, z, y, 0)
+
+    @pl.when(core == 0)
+    def _():
+        pl.semaphore_wait(vouch.at[4], 1)
+
+    each((4, 3, 5), line_kv)
+    each(LINE, line_q)
     each(LINE, line_w)
     each(LINE, line_cq)
 
@@ -340,7 +356,7 @@
     each(LINE, line_out)
     local(out_rows.at[rows(z * TOK, TOK), :], out_ref.at[:, head_columns(z)], rs.at[11])
 
-    wait_bytes(slots_far, ss.at[0])
+    wait_bytes(slots_a, ss.at[0])
     wait_bytes(kv.at[0, :, pl.ds(0, 224), :], ss.at[1])
     wait_bytes(queries.at[0, pl.ds(0, 224), :], ss.at[2])
     wait_bytes(queries.at[0, pl.ds(0, 224), :], ss.at[3])

time: 43.8 us -> 42.7 us (0.975)
  Pallas kernels: 41.8 us -> 40.7 us
    pallas_call x1, Pallas kernels: 41.8 us -> 40.7 us  [on_device(): pl.pallas_call(kernel, out_shape=pltpu.VMEM((TOK, HEADS * HEAD_DIM), BF16...]
where the time goes in v5:
time: 42.7 us; the launch traced here: 42.6 us
  Pallas kernels  40.7 us (95%)
  between operations  1.3 us (3%)
  local copies, waits for them, and re-layouts  0.63 us (1%)
    pallas_call x1, Pallas kernels, on_device(): pl.pallas_call(kernel, out_shape=pltpu.VMEM((TOK, HEADS * HEAD_DIM), BF16...  40.7 us

profile of v5, /device:TPU:1, one launch (start us, length us, event | category | flops | bytes accessed | tf_op | source)
XLA Modules:
  0.0 42.6 jit_solution(5407412705028379986)
XLA Ops:
  1.3 40.7 %shard_map.82 = bf16[32,1024]{1,0:T(8,128)(2,1)S(1)} custom-call(s32[1]{0:T(128)S(6)} %copy.11.owner_ref, s32[1]{0:T(128)S(6)} %copy.12.len_ref, bf16[32,1024]{1,0:T(8,128)(2,1)} %q_hbm.1, bf16[32,1024]{1,0:T(8,128)(2,1)} %k_hbm.1, bf16[32,1024]{1,0:T(8,128)(2,1)} %v_hbm.1, bf16[32,1024]{1,0:T(8,128)(2,1)} %cq_hbm.1, bf16[1,128,4096]{2,1,0:T(8,128)(2,1)} %text_hbm.1, ...), custom_call_target="tpu_custom_call" | custom-call | flops 700000000 | bytes 2000000 | tf_op jit(solution)/shard_map/pallas_call | solution.py:381
  42.0 0.6 %copy.10 = bf16[32,1024]{1,0:T(8,128)(2,1)} copy(bf16[32,1024]{1,0:T(8,128)(2,1)S(1)} %shard_map.82) | data formatting | bytes 131072

commit v6 on v5

--- a/solution.py
+++ b/solution.py
@@ -333,27 +333,33 @@
     top = jnp.maximum(jnp.maximum(tops[0], tops[1]), jnp.maximum(tops[2], tops[3]))
     shares = [stats[s, 1:2, :] * jnp.exp2((tops[s] - top) * SCALE) for s in range(NX * NC)]
     whole = 1.0 / (shares[0] + shares[1] + shares[2] + shares[3])
-    mixed[...] = sum(accs[s].astype(F32) * (shares[s] * whole) for s in range(NX * NC))
+    mixed[...] = sum(accs[s].astype(F32) * (shares[s] * whole) for s in range(NX * NC)).T
 
     wait_bytes(cross_q, rs.at[3])
     wait_bytes(cross_q.at[pl.ds(0, 240), :], rs.at[12])
     cross = cross_kv[...].astype(F32)
     cross_keys = cross[:, :, :8].reshape(NC * HALF, HEAD_DIM).astype(BF16)
     cross_values = cross[:, :, 8:].reshape(NC * HALF, HEAD_DIM).astype(BF16)
-    scores = dot_last(cross_keys, cross_q[...])
-    valid = lax.broadcasted_iota(jnp.int32, scores.shape, 0) < len_ref[0]
-    scores = jnp.where(valid, scores, -1e30)
-    weights = jnp.exp2((scores - jnp.max(scores, axis=0, keepdims=True)) * SCALE)
-    total = jnp.sum(weights, axis=0, keepdims=True)
-    result = mixed[...] + dot_first(cross_values, weights.astype(BF16)) * (1.0 / total)
-    out_rows[...] = result.T.astype(BF16)
-
-
-    def line_out(t):
+    cross_values = cross_values.T
+    valid = lax.broadcasted_iota(jnp.int32, (NC * HALF, 4 * TOK), 0) < len_ref[0]
+
+    def send_out(t):
         zz = (z + t) % NZ
         send(out_rows.at[rows(zz * TOK, TOK), :], out_ref.at[:, head_columns(z)], ss.at[15], rs.at[11], x, zz, y, core)
 
-    each(LINE, line_out)
+    for steps in ((4, 3, 5, 2), (6, 1, 7, 0)):
+        places = [rows((z + t) % NZ * TOK, TOK) for t in steps]
+        scores = dot_last(cross_keys, jnp.concatenate([cross_q[place, :] for place in places], axis=0))
+        scores = jnp.where(valid, scores, -1e30)
+        weights = jnp.exp2((scores - jnp.max(scores, axis=0, keepdims=True)) * SCALE)
+        total = jnp.sum(weights, axis=0, keepdims=True)
+        crossed = jnp.dot(cross_values, weights.astype(BF16), preferred_element_type=F32) * (1.0 / total)
+        crossed = crossed.T
+        for i, place in enumerate(places):
+            out_rows[place, :] = (mixed[place, :] + crossed[i * TOK : (i + 1) * TOK]).astype(BF16)
+        for t in steps:
+            if t:
+                send_out(t)
     local(out_rows.at[rows(z * TOK, TOK), :], out_ref.at[:, head_columns(z)], rs.at[11])
 
     wait_bytes(slots_a, ss.at[0])
@@ -399,7 +405,7 @@
             pltpu.VMEM((PLANE, 2, 8, HEAD_DIM), F32),
             pltpu.VMEM((PLANE, 2, 8, HEAD_DIM), F32),
             pltpu.VMEM((NC, PLANE, 16, HEAD_DIM), BF16),
-            pltpu.VMEM((HEAD_DIM, SLOT), F32),
+            pltpu.VMEM((SLOT, HEAD_DIM), F32),
             pltpu.VMEM((NX * NC, HEAD_DIM, SLOT), BF16),
             pltpu.VMEM((NX * NC, HEAD_DIM, SLOT), BF16),
             pltpu.VMEM((NX * NC, 8, SLOT), F32),

time: 42.7 us -> 42.6 us (level)
  no operation moved by 1% of the time
where the time goes in v6:
time: 42.6 us; the launch traced here: 42.5 us
  Pallas kernels  40.6 us (95%)
  between operations  1.3 us (3%)
  local copies, waits for them, and re-layouts  0.63 us (1%)
    pallas_call x1, Pallas kernels, on_device(): pl.pallas_call(kernel, out_shape=pltpu.VMEM((TOK, HEADS * HEAD_DIM), BF16...  40.6 us

profile of v6, /device:TPU:1, one launch (start us, length us, event | category | flops | bytes accessed | tf_op | source)
XLA Modules:
  0.0 42.5 jit_solution(12077452827517927254)
XLA Ops:
  1.3 40.6 %shard_map.82 = bf16[32,1024]{1,0:T(8,128)(2,1)S(1)} custom-call(s32[1]{0:T(128)S(6)} %copy.11.owner_ref, s32[1]{0:T(128)S(6)} %copy.12.len_ref, bf16[32,1024]{1,0:T(8,128)(2,1)} %q_hbm.1, bf16[32,1024]{1,0:T(8,128)(2,1)} %k_hbm.1, bf16[32,1024]{1,0:T(8,128)(2,1)} %v_hbm.1, bf16[32,1024]{1,0:T(8,128)(2,1)} %cq_hbm.1, bf16[1,128,4096]{2,1,0:T(8,128)(2,1)} %text_hbm.1, ...), custom_call_target="tpu_custom_call" | custom-call | flops 700000000 | bytes 2000000 | tf_op jit(solution)/shard_map/pallas_call | solution.py:387
  41.9 0.6 %copy.10 = bf16[32,1024]{1,0:T(8,128)(2,1)} copy(bf16[32,1024]{1,0:T(8,128)(2,1)S(1)} %shard_map.82) | data formatting | bytes 131072

commit v7 on v6

--- a/solution.py
+++ b/solution.py
@@ -142,24 +142,17 @@
     def _():
         pl.semaphore_wait(barrier, 17)
 
+    @pl.when(core == 1)
+    def _():
+        greet(vouch.at[0], x, z, y, 0)
+        greet(vouch.at[1], 1 - x, z, y, 1)
+        for t in (2, 6):
+            greet(vouch.at[2], x, (z + t) % NZ, y, 1)
+
     theirs = rows(other * 64, 64)
     for i in range(NX):
         columns = half(x, i)
         send(text_hbm.at[0, theirs, columns], halves_of[i].at[core], ss.at[0], halves.at[i], x, z, y, other)
-
-    @pl.when(core == 1)
-    def _():
-        greet(vouch.at[0], x, z, y, 0)
-        greet(vouch.at[1], 1 - x, z, y, 1)
-        for t in (2, 6):
-            greet(vouch.at[2], x, (z + t) % NZ, y, 1)
-
-    local(k_hbm.at[:, head_columns(z)], kv.at[y, 0, rows(z * TOK, TOK), :], rs.at[1])
-    local(v_hbm.at[:, head_columns(z)], kv.at[y, 1, rows(z * TOK, TOK), :], rs.at[1])
-    local(q_hbm.at[:, head_columns(z)], queries.at[xc, rows(z * TOK, TOK), :], rs.at[2])
-    local(cq_hbm.at[:, head_columns(z)], cross_q.at[rows(z * TOK, TOK), :], rs.at[3])
-    for j in range(2):
-        local(w_hbm.at[:, head_columns(j * HEADS + z)], weight.at[j, z, core], rs.at[4])
 
     def line_kv(t):
         zz = (z + t) % NZ
@@ -208,6 +201,13 @@
             send_piece(px * NY + (y + step) % NY)
     local(piece_out.at[f], pieces.at[f], rs.at[5])
 
+    local(k_hbm.at[:, head_columns(z)], kv.at[y, 0, rows(z * TOK, TOK), :], rs.at[1])
+    local(v_hbm.at[:, head_columns(z)], kv.at[y, 1, rows(z * TOK, TOK), :], rs.at[1])
+    local(q_hbm.at[:, head_columns(z)], queries.at[xc, rows(z * TOK, TOK), :], rs.at[2])
+    local(cq_hbm.at[:, head_columns(z)], cross_q.at[rows(z * TOK, TOK), :], rs.at[3])
+    for j in range(2):
+        local(w_hbm.at[:, head_columns(j * HEADS + z)], weight.at[j, z, core], rs.at[4])
+
     each((2, 6, 1, 7), line_kv)
 
     @pl.when(core == 1)
@@ -234,7 +234,6 @@
     each((4, 3, 5), line_kv)
     each(LINE, line_q)
     each(LINE, line_w)
-    each(LINE, line_cq)
 
     wait_bytes(kv.at[0], rs.at[1])
     for t in (2, 1, 3):
@@ -307,6 +306,7 @@
         send(part_out.at[p], parts.at[f], ss.at[12], rs.at[10], px, z, py, core)
 
     each(ACROSS, plane_parts)
+    each(LINE, line_cq)
     parts[f] = part_out[f]
 
     acc, top, total = self_part(xc)

time: 42.6 us -> 42.7 us (level)
  no operation moved by 1% of the time
where the time goes in v7:
time: 42.7 us; the launch traced here: 42.6 us
  Pallas kernels  40.7 us (95%)
  between operations  1.3 us (3%)
  local copies, waits for them, and re-layouts  0.63 us (1%)
    pallas_call x1, Pallas kernels, on_device(): pl.pallas_call(kernel, out_shape=pltpu.VMEM((TOK, HEADS * HEAD_DIM), BF16...  40.7 us

profile of v7, /device:TPU:1, one launch (start us, length us, event | category | flops | bytes accessed | tf_op | source)
XLA Modules:
  0.0 42.6 jit_solution(8465142861784951380)
XLA Ops:
  1.3 40.7 %shard_map.82 = bf16[32,1024]{1,0:T(8,128)(2,1)S(1)} custom-call(s32[1]{0:T(128)S(6)} %copy.11.owner_ref, s32[1]{0:T(128)S(6)} %copy.12.len_ref, bf16[32,1024]{1,0:T(8,128)(2,1)} %q_hbm.1, bf16[32,1024]{1,0:T(8,128)(2,1)} %k_hbm.1, bf16[32,1024]{1,0:T(8,128)(2,1)} %v_hbm.1, bf16[32,1024]{1,0:T(8,128)(2,1)} %cq_hbm.1, bf16[1,128,4096]{2,1,0:T(8,128)(2,1)} %text_hbm.1, ...), custom_call_target="tpu_custom_call" | custom-call | flops 700000000 | bytes 2000000 | tf_op jit(solution)/shard_map/pallas_call | solution.py:387
  42.0 0.6 %copy.10 = bf16[32,1024]{1,0:T(8,128)(2,1)} copy(bf16[32,1024]{1,0:T(8,128)(2,1)S(1)} %shard_map.82) | data formatting | bytes 131072
